TPU v7x, 128 devices: a whole 4x4x4 slice. The times are simulated.
128 devices in a mesh: branch: 16 (over y, x), tensor: 8 (over z, core).
Axes of the slice: x: 4, y: 4, z: 4, core: 2. Of those that a mesh axis runs over, the one named last changes fastest.
Arguments:
- queries: bfloat16 [4096, 8192], P('branch', 'tensor'), may hold values from -6 to 6
- keys: bfloat16 [4096, 1024], P('branch', 'tensor'), may hold values from -6 to 6
- values: bfloat16 [4096, 1024], P('branch', 'tensor'), may hold values from -6 to 6
- grad_out: bfloat16 [4096, 8192], P('branch', 'tensor'), may hold values from -6 to 6
- w_out: bfloat16 [8192, 8192], P('tensor'), may hold values from -0.0625 to 0.0625
- parent: int32 [16], replicated, may hold values from -1 to 14, as said below
Outputs:
- attn_out: bfloat16 [4096, 8192], P('branch', 'tensor')
- grad_queries: bfloat16 [4096, 8192], P('branch', 'tensor')
- grad_keys: bfloat16 [4096, 1024], P('branch', 'tensor')
- grad_values: bfloat16 [4096, 1024], P('branch', 'tensor')
Inputs may be any that keep to these rules, and one draw needn't show every extreme that they name: parent of node 0 is -1; every other node's parent has a smaller index; the last node's parent is node 14.
All inputs are finite; a program needn't handle non-finite values.
Results may differ from a plain program's by a relative error of at most 0.04.
Values may be sent and summed in bfloat16 or wider, within the bound.
No kernel may reach another device: no remote copies, remote signals or barrier semaphores. Data moves between devices by JAX's collectives and lax.ppermute only.
A program may use at most 256 MiB of HBM per device.

v0:
```python
import math

import jax
import jax.numpy as jnp
from jax import lax
from jax.sharding import PartitionSpec as P

HEAD_DIM = 128


NEG_FLOOR = -1e30


def ancestor_table(parent, node_count):
    indices = jnp.arange(node_count, dtype=jnp.int32)

    def climb_up(state_now, unused):
        current, marked = state_now
        onehot = current[:, None] == indices[None, :]
        marked = jnp.logical_or(marked, onehot)
        upward = jnp.sum(jnp.where(onehot, parent[None, :], 0), axis=1)
        upward = jnp.where(current >= 0, upward, -1)
        return ((upward, marked), None)

    start_state = (parent, jnp.zeros((node_count, node_count), dtype=jnp.bool_))
    (unused_last, marked), unused_out = lax.scan(climb_up, start_state, None, length=node_count)
    return marked


def per_device(queries, keys, values, grad_out, w_out, parent):
    seg_len = queries.shape[0]
    node_count = lax.axis_size("branch")
    own_node = lax.axis_index("branch")
    head_dim = HEAD_DIM
    kv_local = keys.shape[1] // head_dim
    heads_local = queries.shape[1] // head_dim
    group_size = heads_local // kv_local
    score_scale = 1.0 / math.sqrt(head_dim)
    marked = ancestor_table(parent, node_count)
    node_ids = jnp.arange(node_count, dtype=jnp.int32)
    own_hot = node_ids == own_node
    own_ancestors = jnp.any(jnp.logical_and(marked, own_hot[:, None]), axis=0)
    positions = jnp.arange(seg_len, dtype=jnp.int32)
    causal = positions[None, :] <= positions[:, None]
    gathered_keys, gathered_values = (
        lax.all_gather(keys, "branch", axis=0, tiled=True),
        lax.all_gather(values, "branch", axis=0, tiled=True),
    )
    head_grads = jnp.einsum(
        "rn,hn->rh",
        lax.all_gather(grad_out, "tensor", axis=1, tiled=True),
        w_out,
        preferred_element_type=jnp.float32,
    ).astype(jnp.bfloat16)
    query4 = queries.reshape(seg_len, kv_local, group_size, head_dim)
    grad4 = head_grads.reshape(seg_len, kv_local, group_size, head_dim)

    def block_of(node_index):
        first_row = node_index * seg_len
        key_block = lax.dynamic_slice_in_dim(gathered_keys, first_row, seg_len, 0).reshape(
            seg_len, kv_local, head_dim
        )
        value_block = lax.dynamic_slice_in_dim(gathered_values, first_row, seg_len, 0).reshape(
            seg_len, kv_local, head_dim
        )
        is_ancestor = jnp.any(jnp.logical_and(own_ancestors, node_ids == node_index))
        is_self = node_index == own_node
        visible = jnp.logical_or(is_ancestor, jnp.logical_and(is_self, causal))
        active = jnp.logical_or(is_ancestor, is_self)
        scores = (
            jnp.einsum("rcgd,kcd->cgrk", query4, key_block, preferred_element_type=jnp.float32)
            * score_scale
        )
        return (key_block, value_block, visible, active, scores)

    def max_pass(node_index, state_now):
        key_block, value_block, visible, active, scores = block_of(node_index)
        row_max, row_sum = state_now
        masked = jnp.where(visible[None, None], scores, -jnp.inf)
        next_max = jnp.maximum(row_max, jnp.max(masked, axis=3))
        next_sum = row_sum * jnp.exp(row_max - next_max) + jnp.sum(
            jnp.exp(masked - next_max[..., None]), axis=3
        )
        return (next_max, next_sum)

    initial = (
        jnp.full((kv_local, group_size, seg_len), NEG_FLOOR, jnp.float32),
        jnp.zeros((kv_local, group_size, seg_len), jnp.float32),
    )
    row_max, row_sum = lax.fori_loop(0, node_count, max_pass, initial)
    log_total = row_max + jnp.log(row_sum)

    def out_pass(node_index, state_now):
        key_block, value_block, visible, active, scores = block_of(node_index)
        masked = jnp.where(visible[None, None], scores, -jnp.inf)
        attention_b = jnp.exp(masked - log_total[..., None]).astype(jnp.bfloat16)
        return state_now + jnp.einsum(
            "cgrk,kcd->cgrd", attention_b, value_block, preferred_element_type=jnp.float32
        )

    attended = lax.fori_loop(
        0, node_count, out_pass, jnp.zeros((kv_local, group_size, seg_len, head_dim), jnp.float32)
    )
    attn_out = (
        attended.transpose(2, 0, 1, 3).reshape(seg_len, heads_local * head_dim).astype(jnp.bfloat16)
    )
    attended4 = attn_out.reshape(seg_len, kv_local, group_size, head_dim).astype(jnp.float32)
    row_delta = jnp.sum(grad4.astype(jnp.float32) * attended4, axis=3).transpose(1, 2, 0)
    term_rows = node_count * seg_len

    def back_pass(node_index, state_now):
        key_block, value_block, visible, active, scores = block_of(node_index)
        query_grad, key_terms = state_now
        masked = jnp.where(visible[None, None], scores, -jnp.inf)
        attention = jnp.exp(masked - log_total[..., None])
        attention_b = attention.astype(jnp.bfloat16)
        dprobs = jnp.einsum(
            "rcgd,kcd->cgrk", grad4, value_block, preferred_element_type=jnp.float32
        )
        dscores = (attention * (dprobs - row_delta[..., None])).astype(jnp.bfloat16)
        query_grad = (
            query_grad
            + jnp.einsum("cgrk,kcd->rcgd", dscores, key_block, preferred_element_type=jnp.float32)
            * score_scale
        )
        key_part = (
            jnp.einsum("cgrk,rcgd->kcd", dscores, query4, preferred_element_type=jnp.float32)
            * score_scale
        )
        value_part = jnp.einsum(
            "cgrk,rcgd->kcd", attention_b, grad4, preferred_element_type=jnp.float32
        )
        joined = jnp.concatenate(
            [
                key_part.reshape(seg_len, kv_local * head_dim),
                value_part.reshape(seg_len, kv_local * head_dim),
            ],
            axis=1,
        )
        key_terms = lax.dynamic_update_slice_in_dim(
            key_terms, joined, (node_index * seg_len).astype(jnp.int32), 0
        )
        return (query_grad, key_terms)

    initial_back = (
        jnp.zeros((seg_len, kv_local, group_size, head_dim), jnp.float32),
        jnp.zeros((term_rows, 2 * kv_local * head_dim), jnp.float32),
    )
    query_grad, key_terms = lax.fori_loop(0, node_count, back_pass, initial_back)
    grad_queries = query_grad.reshape(seg_len, heads_local * head_dim).astype(jnp.bfloat16)
    own_terms = lax.psum_scatter(key_terms, "branch", scatter_dimension=0, tiled=True)
    grad_keys = own_terms[:, : kv_local * head_dim].astype(jnp.bfloat16)
    grad_values = own_terms[:, kv_local * head_dim :].astype(jnp.bfloat16)
    return (attn_out, grad_queries, grad_keys, grad_values)


def solution(mesh):
    return jax.shard_map(
        per_device,
        mesh=mesh,
        in_specs=(
            P("branch", "tensor"),
            P("branch", "tensor"),
            P("branch", "tensor"),
            P("branch", "tensor"),
            P("tensor", None),
            P(),
        ),
        out_specs=(
            P("branch", "tensor"),
            P("branch", "tensor"),
            P("branch", "tensor"),
            P("branch", "tensor"),
        ),
        check_vma=False,
    )
```

profile of v0, /device:TPU:0, one launch (start us, length us, event | category | flops | bytes accessed | tf_op | source)
XLA Modules:
  0.0 377.9 jit_solution(1623329179172721584)
XLA Ops:
  10.1 15.1 %while.59 = (s32[]{:T(128)}, s32[16]{0:T(128)S(1)}, pred[16,16]{1,0:T(8,128)(4,1)S(1)}, s32[16]{0:T(128)}, s32[]{:T(128)}, /*index=5*/s32[]{:T(128)}) while((s32[]{:T(128)}, s32[16]{0:T(128)S(1)}, pred[16,16]{1,0:T(8,128)(4,1)S(1)}, s32[16]{0:T(128)}, s32[]{:T(128)}, /*index=5*/s32[]{:T(128)}) %tuple.115), condition=%wide.region_2.3_spmd.clone, body=%wide.region_0.2_spmd.clone.sunk | while | flops 1555 | bytes 1039 | solution.py:26
  26.9 28.4 %all-gather.4.cloned.1.call-done = bf16[4096,128]{1,0:T(8,128)(2,1)} async-done(((bf16[256,128]{1,0:T(8,128)(2,1)}), bf16[4096,128]{1,0:T(8,128)(2,1)}) %all-gather.4.cloned.1.call-update) | async-done | bytes 1048592 | tf_op jit(solution)/shard_map/all_gather | solution.py:46
  55.2 50.3 %while.60 = (s32[]{:T(128)}, f32[1,8,256]{2,1,0:T(8,128)S(1)}, f32[1,8,256]{2,1,0:T(8,128)S(1)}, pred[16]{0:T(512)(128)(4,1)S(1)}, s32[]{:T(128)}, /*index=5*/bf...) while((s32[]{:T(128)}, f32[1,8,256]{2,1,0:T(8,128)S(1)}, ...), condition=%wide.region_8.9_spmd.clone, body=%wide.region_4.8_spmd.clone.sunk | while | flops 138094640 | bytes 5087442 | solution.py:90
  59.7 1.3 fusion.106
  62.8 1.3 fusion.106
  72.3 1.3 fusion.106
  78.6 1.3 fusion.106
  88.0 1.3 fusion.106
  100.6 1.3 fusion.106
  103.7 1.3 fusion.106
  105.6 55.2 %while.61 = (s32[]{:T(128)}, f32[1,8,256,128]{3,2,1,0:T(8,128)S(1)}, pred[16]{0:T(512)(128)(4,1)S(1)}, s32[]{:T(128)}, bf16[4096,128]{1,0:T(8,128)(2,1)}, /*inde...) while((s32[]{:T(128)}, ...), condition=%wide.region_11.12_spmd.clone, body=%wide.region_9.11_spmd.clone.sunk | while | flops 271253568 | bytes 2893524 | solution.py:101
  106.9 2.1 fusion.111
  110.4 2.2 fusion.111
  113.9 2.1 fusion.111
  117.3 2.1 fusion.111
  120.8 2.1 fusion.111
  124.2 2.1 fusion.111
  127.7 2.1 fusion.111
  131.1 2.1 fusion.111
  134.6 2.1 fusion.111
  138.0 2.1 fusion.111
  141.5 2.1 fusion.111
  144.9 2.1 fusion.111
  148.4 2.1 fusion.111
  151.8 2.1 fusion.111
  155.3 2.1 fusion.111
  158.7 2.1 fusion.111
  161.8 11.6 %fusion.73 = bf16[32,8,8,128]{3,1,2,0:T(8,128)(2,1)S(1)} fusion(bf16[256,8192]{1,0:T(8,128)(2,1)} %all-gather.8.cloned.1.call-done, bf16[1024,8192]{1,0:T(8,128)(2,1)} %param.18), kind=kOutput, calls=%fused_computation.85 | convolution fusion | flops 4295229440 | bytes 21495808 | tf_op jit(solution)/shard_map/rn,hn->rh/dot_general | solution.py:49
  173.9 1.6 multiply_reduce_fusion
  175.4 2.2 broadcast_in_dim.130.clone
  177.6 115.2 %while.62 = (s32[]{:T(128)}, f32[256,1,8,128]{0,3,2,1:T(8,128)S(1)}, f32[4096,256]{1,0:T(8,128)}, bf16[4096,128]{1,0:T(8,128)(2,1)}, pred[16]{0:T(512)(128)(4,1)...) while((s32[]{:T(128)}, ...), condition=%wide.region_15.16_spmd.clone, body=%wide.region_13.15_spmd.clone.sunk | while | flops 675840064 | bytes 15810813 | solution.py:149
  179.0 1.4 fusion.123
  182.6 1.3 fusion.125
  186.1 1.4 fusion.123
  189.8 1.3 fusion.125
  193.3 1.4 fusion.123
  197.0 1.3 fusion.125
  200.5 1.4 fusion.123
  204.2 1.3 fusion.125
  207.7 1.4 fusion.123
  211.4 1.3 fusion.125
  214.9 1.4 fusion.123
  218.6 1.3 fusion.125
  222.1 1.4 fusion.123
  225.8 1.3 fusion.125
  229.3 1.4 fusion.123
  233.0 1.3 fusion.125
  236.5 1.4 fusion.123
  240.2 1.3 fusion.125
  243.7 1.4 fusion.123
  247.4 1.3 fusion.125
  250.9 1.4 fusion.123
  254.6 1.3 fusion.125
  258.1 1.4 fusion.123
  261.8 1.3 fusion.125
  265.3 1.4 fusion.123
  269.0 1.3 fusion.125
  272.5 1.4 fusion.123
  276.2 1.3 fusion.125
  279.7 1.4 fusion.123
  283.4 1.3 fusion.125
  286.9 1.4 fusion.123
  290.6 1.3 fusion.125
  295.1 74.6 %reduce-scatter.2.cloned.1.call-done = f32[256,256]{1,0:T(8,128)} async-done(((f32[4096,256]{1,0:T(8,128)}), f32[256,256]{1,0:T(8,128)}) %reduce-scatter.2.cloned.1.call-update) | async-done | bytes 262160 | tf_op jit(solution)/shard_map/reduce_scatter | solution.py:151
  (344 shorter events, 156.5 us)
Async XLA Ops:
  7.2 48.1 %all-gather.4.cloned.1.call-start = ((), (), s32[]{:S(2)}) async-start(), calls=%async_computation.1 | async-start | bytes 1114112 | tf_op jit(solution)/shard_map/all_gather | solution.py:46
  7.9 97.7 %all-gather.6.cloned.1.call-start = ((), (), s32[]{:S(2)}) async-start(), calls=%async_computation.2 | async-start | bytes 1114112 | tf_op jit(solution)/shard_map/all_gather | solution.py:47
  8.6 152.2 %all-gather.8.cloned.1.call-start = ((), (), s32[]{:S(2)}) async-start(), calls=%async_computation.3 | async-start | bytes 4718592 | tf_op jit(solution)/shard_map/all_gather | solution.py:51
  9.4 360.3 %reduce-scatter.2.cloned.1.call-start = ((), (), s32[]{:S(2)}) async-start(), calls=%async_computation.4 | async-start | bytes 4456448 | tf_op jit(solution)/shard_map/reduce_scatter | solution.py:151
  160.8 1.0 copy-start
Sparse Core Ops, SparseCore 0:
  10.1 45.0 all-gather.3
  57.4 41.8 all-gather.5
  100.9 31.5 all-gather.7
  293.0 76.7 reduce-scatter.1
where the time goes:
time: 382 us; the launch traced here: 378 us
  matrix products  145 us (38%)
  waiting for transfers between devices  105 us (27%)
  other arithmetic  88.4 us (23%)
  local copies, waits for them, and re-layouts  22.5 us (6%)
  between operations  13.9 us (4%)
    reduce_scatter x1, waiting for transfers between devices, per_device(): lax.psum_scatter(key_terms, 'branch', scatter_dimension=0, tiled=True)  74.6 us
    dot_general x32, matrix products, block_of(): jnp.einsum('rcgd,kcd->cgrk', query4, key_block, preferred_element_type=jn...  43.3 us
    dot_general x16, matrix products, out_pass(): jnp.einsum('cgrk,kcd->cgrd', attention_b, value_block, preferred_element_...  33.5 us
    or x48, other arithmetic, block_of(): visible = jnp.logical_or(is_ancestor, jnp.logical_and(is_self, causal))  32.6 us
    reduce_or x48, other arithmetic, block_of(): jnp.any(jnp.logical_and(own_ancestors, node_ids == node_index))  30.4 us
    all_gather x1, waiting for transfers between devices, per_device(): lax.all_gather(keys, 'branch', axis=0, tiled=True)  28.4 us
    dot_general x16, matrix products, back_pass(): jnp.einsum('cgrk,kcd->rcgd', dscores, key_block, preferred_element_type=j...  21 us
    dot_general x16, matrix products, back_pass(): jnp.einsum('rcgd,kcd->cgrk', grad4, value_block, preferred_element_type=j...  20.3 us
  transfers between devices with their start and end apart: 4, of which 2 were waited for; matrix products, arithmetic and copies ran while one was open for 33% of the time, Pallas kernels for 0%

commit v1 on v0

v1 whole, which is shorter than its diff:
```python
import math

import jax
import jax.numpy as jnp
from jax import lax
from jax.experimental import pallas as pl
from jax.experimental.pallas import tpu as pltpu
from jax.sharding import PartitionSpec as P

HEAD_DIM = 128
SEG = 256
NODES = 16
GROUP = 8
SCALE = 1.0 / math.sqrt(HEAD_DIM)
EXP2_SCALE = SCALE * math.log2(math.e)
NEG_FLOOR = -1e30
VMEM_LIMIT = 48 * 1024 * 1024

NT = (((1,), (1,)), ((), ()))
NN = (((1,), (0,)), ((), ()))


def matmul(left, right, dims=NN):
    return lax.dot_general(left, right, dims, preferred_element_type=jnp.float32)


def list_visible(parent_ref, own, visible_ref):
    visible_ref[0] = own

    def climb(state):
        node, count = state
        above = parent_ref[node]
        visible_ref[count] = above
        return above, count + 1

    def has_parent(state):
        node, count = state
        return jnp.logical_and(parent_ref[node] >= 0, count < NODES)

    return lax.while_loop(has_parent, climb, (own, jnp.int32(1)))[1]


def forward_kernel(
    parent_ref, q_ref, kv_ref, out_ref, factor_ref, weights_hbm,
    visible_ref, kv_buf, weights_buf, acc_ref, max_ref, sum_ref, seen_max_ref, kv_sem, weights_sem,
):
    own = lax.axis_index("branch")
    count = list_visible(parent_ref, own, visible_ref)

    def kv_copy(i):
        return pltpu.make_async_copy(kv_ref.at[visible_ref[i]], kv_buf.at[i], kv_sem.at[i])

    def weights_copy(i):
        return pltpu.make_async_copy(weights_buf.at[i], weights_hbm.at[i], weights_sem.at[i])

    def start_kv(i, unused):
        kv_copy(i).start()
        return unused

    lax.fori_loop(0, count, start_kv, 0)

    def block(i, is_own):
        kv_copy(i).wait()
        keys = kv_buf[i, :, :HEAD_DIM]
        values_t = kv_buf[i, :, HEAD_DIM:].astype(jnp.float32).T.astype(jnp.bfloat16)
        for h in range(GROUP):
            rows = pl.ds(h * SEG, SEG)
            scores = matmul(keys, q_ref[:, h * HEAD_DIM : (h + 1) * HEAD_DIM], NT)
            if is_own:
                key_pos = lax.broadcasted_iota(jnp.int32, (SEG, SEG), 0)
                row_pos = lax.broadcasted_iota(jnp.int32, (SEG, SEG), 1)
                scores = jnp.where(key_pos <= row_pos, scores, NEG_FLOOR)
            block_max = jnp.max(scores, axis=0, keepdims=True)
            if is_own:
                new_max = block_max
            else:
                old_max = max_ref[h : h + 1, :]
                new_max = jnp.maximum(old_max, block_max)
            weights = jnp.exp2((scores - new_max) * EXP2_SCALE)
            block_sum = jnp.sum(weights, axis=0, keepdims=True)
            weights_b = weights.astype(jnp.bfloat16)
            weights_buf[i, :, rows] = weights_b
            part = matmul(values_t, weights_b)
            if is_own:
                acc_ref[h] = part
                sum_ref[h : h + 1, :] = block_sum
            else:
                shrink = jnp.exp2((old_max - new_max) * EXP2_SCALE)
                acc_ref[h] = acc_ref[h] * shrink + part
                sum_ref[h : h + 1, :] = sum_ref[h : h + 1, :] * shrink + block_sum
            max_ref[h : h + 1, :] = new_max
        seen_max_ref[i] = max_ref[...]
        weights_copy(i).start()

    block(0, True)

    def ancestor(i, unused):
        block(i, False)
        return unused

    lax.fori_loop(1, count, ancestor, 0)
    inverse = 1.0 / sum_ref[...]
    final_max = max_ref[...]

    def finish(i, unused):
        factor_ref[i] = jnp.exp2((seen_max_ref[i] - final_max) * EXP2_SCALE) * inverse
        return unused

    lax.fori_loop(0, count, finish, 0)
    for h in range(GROUP):
        out = acc_ref[h] * inverse[h : h + 1, :]
        out_ref[:, h * HEAD_DIM : (h + 1) * HEAD_DIM] = out.T.astype(jnp.bfloat16)

    def drain(i, unused):
        weights_copy(i).wait()
        return unused

    lax.fori_loop(0, count, drain, 0)


def forward(parent, queries, kv_all):
    return pl.pallas_call(
        forward_kernel,
        out_shape=(
            jax.ShapeDtypeStruct((SEG, GROUP * HEAD_DIM), jnp.bfloat16),
            jax.ShapeDtypeStruct((NODES, GROUP, SEG), jnp.float32),
            jax.ShapeDtypeStruct((NODES, SEG, GROUP * SEG), jnp.bfloat16),
        ),
        in_specs=[
            pl.BlockSpec(memory_space=pltpu.SMEM),
            pl.BlockSpec(memory_space=pltpu.VMEM),
            pl.BlockSpec(memory_space=pl.ANY),
        ],
        out_specs=(
            pl.BlockSpec(memory_space=pltpu.VMEM),
            pl.BlockSpec(memory_space=pltpu.VMEM),
            pl.BlockSpec(memory_space=pl.ANY),
        ),
        scratch_shapes=[
            pltpu.SMEM((NODES,), jnp.int32),
            pltpu.VMEM((NODES, SEG, 2 * HEAD_DIM), jnp.bfloat16),
            pltpu.VMEM((NODES, SEG, GROUP * SEG), jnp.bfloat16),
            pltpu.VMEM((GROUP, HEAD_DIM, SEG), jnp.float32),
            pltpu.VMEM((GROUP, SEG), jnp.float32),
            pltpu.VMEM((GROUP, SEG), jnp.float32),
            pltpu.VMEM((NODES, GROUP, SEG), jnp.float32),
            pltpu.SemaphoreType.DMA((NODES,)),
            pltpu.SemaphoreType.DMA((NODES,)),
        ],
        compiler_params=pltpu.CompilerParams(vmem_limit_bytes=VMEM_LIMIT),
        cost_estimate=pl.CostEstimate(flops=2 * 10**9, bytes_accessed=8 * 2**20, transcendentals=3 * 10**6),
        name="attend",
    )(parent, queries, kv_all)


def backward_kernel(
    parent_ref, q_ref, grad_ref, out_ref, factor_ref, kv_ref, weights_hbm, dq_ref, dkv_ref,
    visible_ref, kv_buf, weights_buf, dq_acc, delta_ref, kv_sem, weights_sem,
):
    own = lax.axis_index("branch")
    count = list_visible(parent_ref, own, visible_ref)

    def kv_copy(i):
        return pltpu.make_async_copy(kv_ref.at[visible_ref[i]], kv_buf.at[i], kv_sem.at[i])

    def weights_copy(i):
        return pltpu.make_async_copy(weights_hbm.at[i], weights_buf.at[i], weights_sem.at[i])

    def start(i, unused):
        kv_copy(i).start()
        weights_copy(i).start()
        return unused

    lax.fori_loop(0, count, start, 0)
    dkv_ref[...] = jnp.zeros_like(dkv_ref)
    dq_acc[...] = jnp.zeros_like(dq_acc)
    for h in range(GROUP):
        cols = slice(h * HEAD_DIM, (h + 1) * HEAD_DIM)
        products = grad_ref[:, cols].astype(jnp.float32) * out_ref[:, cols].astype(jnp.float32)
        sums = lax.dot_general(
            jnp.ones((GROUP, HEAD_DIM), jnp.float32), products, NT,
            precision=lax.Precision.HIGHEST, preferred_element_type=jnp.float32,
        )
        delta_ref[h : h + 1, :] = sums[0:1, :]

    def block(i, unused):
        kv_copy(i).wait()
        weights_copy(i).wait()
        keys = kv_buf[i, :, :HEAD_DIM]
        values = kv_buf[i, :, HEAD_DIM:]
        keys_t = keys.astype(jnp.float32).T.astype(jnp.bfloat16)
        key_grad = jnp.zeros((SEG, HEAD_DIM), jnp.float32)
        value_grad = jnp.zeros((SEG, HEAD_DIM), jnp.float32)
        for h in range(GROUP):
            cols = slice(h * HEAD_DIM, (h + 1) * HEAD_DIM)
            probs = weights_buf[i, :, pl.ds(h * SEG, SEG)].astype(jnp.float32) * factor_ref[i, h : h + 1, :]
            dprobs = matmul(values, grad_ref[:, cols], NT)
            dscores = (probs * (dprobs - delta_ref[h : h + 1, :])).astype(jnp.bfloat16)
            value_grad = value_grad + matmul(probs.astype(jnp.bfloat16), grad_ref[:, cols])
            key_grad = key_grad + matmul(dscores, q_ref[:, cols])
            dq_acc[h] += matmul(keys_t, dscores)
        node = visible_ref[i]
        dkv_ref[node, :, :HEAD_DIM] = (key_grad * SCALE).astype(jnp.bfloat16)
        dkv_ref[node, :, HEAD_DIM:] = value_grad.astype(jnp.bfloat16)
        return unused

    lax.fori_loop(0, count, block, 0)
    for h in range(GROUP):
        dq_ref[:, h * HEAD_DIM : (h + 1) * HEAD_DIM] = (dq_acc[h] * SCALE).T.astype(jnp.bfloat16)


def backward(parent, queries, head_grads, attn_out, factors, kv_all, weights):
    vmem = pl.BlockSpec(memory_space=pltpu.VMEM)
    hbm = pl.BlockSpec(memory_space=pl.ANY)
    return pl.pallas_call(
        backward_kernel,
        out_shape=(
            jax.ShapeDtypeStruct((SEG, GROUP * HEAD_DIM), jnp.bfloat16),
            jax.ShapeDtypeStruct((NODES, SEG, 2 * HEAD_DIM), jnp.bfloat16),
        ),
        in_specs=[pl.BlockSpec(memory_space=pltpu.SMEM), vmem, vmem, vmem, vmem, hbm, hbm],
        out_specs=(vmem, vmem),
        scratch_shapes=[
            pltpu.SMEM((NODES,), jnp.int32),
            pltpu.VMEM((NODES, SEG, 2 * HEAD_DIM), jnp.bfloat16),
            pltpu.VMEM((NODES, SEG, GROUP * SEG), jnp.bfloat16),
            pltpu.VMEM((GROUP, HEAD_DIM, SEG), jnp.float32),
            pltpu.VMEM((GROUP, SEG), jnp.float32),
            pltpu.SemaphoreType.DMA((NODES,)),
            pltpu.SemaphoreType.DMA((NODES,)),
        ],
        compiler_params=pltpu.CompilerParams(vmem_limit_bytes=VMEM_LIMIT),
        cost_estimate=pl.CostEstimate(flops=4 * 10**9, bytes_accessed=8 * 2**20, transcendentals=0),
        name="attend_grads",
    )(parent, queries, head_grads, attn_out, factors, kv_all, weights)


def per_device(queries, keys, values, grad_out, w_out, parent):
    kv = jnp.concatenate([keys, values], axis=1)
    kv_all = lax.all_gather(kv, "branch", axis=0)
    grad_all = lax.all_gather(grad_out, "tensor", axis=1, tiled=True)
    attn_out, factors, weights = forward(parent, queries, kv_all)
    head_grads = jnp.einsum(
        "rn,hn->rh", grad_all, w_out, preferred_element_type=jnp.float32
    ).astype(jnp.bfloat16)
    grad_queries, dkv = backward(parent, queries, head_grads, attn_out, factors, kv_all, weights)
    own = lax.psum_scatter(
        dkv.reshape(NODES * SEG, 2 * HEAD_DIM), "branch", scatter_dimension=0, tiled=True
    )
    return attn_out, grad_queries, own[:, :HEAD_DIM], own[:, HEAD_DIM:]


def solution(mesh):
    return jax.shard_map(
        per_device,
        mesh=mesh,
        in_specs=(
            P("branch", "tensor"),
            P("branch", "tensor"),
            P("branch", "tensor"),
            P("branch", "tensor"),
            P("tensor", None),
            P(),
        ),
        out_specs=(P("branch", "tensor"),) * 4,
        check_vma=False,
    )
```

time: 382 us -> 204 us (0.53); the launches traced: 378 us -> 204 us
  matrix products: 145 us -> 12.4 us
  other arithmetic: 88.4 us -> 1.54 us
  waiting for transfers between devices: 105 us -> 159 us
  local copies, waits for them, and re-layouts: 22.5 us -> 7.21 us
  Pallas kernels: 0 us -> 10.2 us
    dot_general x113 -> x1, matrix products: 145 us -> 12.4 us  [per_device(): jnp.einsum('rn,hn->rh', grad_all, w_out, preferred_element_type=jnp.float32)]
    all_gather x3 -> x2, waiting for transfers between devices: 28.4 us -> 73.5 us  [the longest x1 48.4 us: per_device(): kv_all = lax.all_gather(kv, 'branch', axis=0)]
    or x64 -> x0, other arithmetic: 34 us -> none  [the longest x48 32.6 us: block_of(): visible = jnp.logical_or(is_ancestor, jnp.logical_and(is_self, causal))]
    reduce_or x49 -> x0, other arithmetic: 30.5 us -> none  [the longest x48 30.4 us: block_of(): jnp.any(jnp.logical_and(own_ancestors, node_ids == node_index))]
    reduce_sum x33 -> x0, other arithmetic: 22.1 us -> none  [the longest x16 13.4 us: climb_up(): upward = jnp.sum(jnp.where(onehot, parent[None, :], 0), axis=1)]
    dynamic_update_slice x32 -> x0, local copies, waits for them, and re-layouts: 13.8 us -> none  [back_pass(): lax.dynamic_update_slice_in_dim(key_terms, joined, (node_index * seg_len)...]
    pallas_call x0 -> x2, Pallas kernels: none -> 10.2 us  [the longest x1 5.2 us: backward(): pl.pallas_call(backward_kernel, out_shape=(jax.ShapeDtypeStruct((SEG, GRO...]
    reduce_scatter x1, waiting for transfers between devices: 74.6 us -> 84.3 us  [per_device(): lax.psum_scatter(dkv.reshape(NODES * SEG, 2 * HEAD_DIM), 'branch', scatte...]
  transfers between devices with their start and end apart: 4 -> 3, of which waited for: 2 -> 3; matrix products, arithmetic and copies ran while one was open for 33% -> 0% of each run, Pallas kernels for 0% -> 2%
where the time goes in v1:
time: 204 us
  waiting for transfers between devices  159 us (78%)
  between operations  13.8 us (7%)
  matrix products  12.4 us (6%)
  Pallas kernels  10.2 us (5%)
  local copies, waits for them, and re-layouts  7.21 us (4%)
    reduce_scatter x1, waiting for transfers between devices, per_device(): lax.psum_scatter(dkv.reshape(NODES * SEG, 2 * HEAD_DIM), 'branch', scatte...  84.3 us
    all_gather x1, waiting for transfers between devices, per_device(): kv_all = lax.all_gather(kv, 'branch', axis=0)  48.4 us
    all_gather x1, waiting for transfers between devices, per_device(): grad_all = lax.all_gather(grad_out, 'tensor', axis=1, tiled=True)  25.1 us
    dot_general x1, matrix products, per_device(): jnp.einsum('rn,hn->rh', grad_all, w_out, preferred_element_type=jnp.float32)  12.4 us
    unnamed x18, local copies, waits for them, and re-layouts  5.68 us
    pallas_call x1, Pallas kernels, backward(): pl.pallas_call(backward_kernel, out_shape=(jax.ShapeDtypeStruct((SEG, GRO...  5.2 us
    pallas_call x1, Pallas kernels, forward(): pl.pallas_call(forward_kernel, out_shape=(jax.ShapeDtypeStruct((SEG, GROU...  4.99 us
  transfers between devices with their start and end apart: 3, of which 3 were waited for; matrix products, arithmetic and copies ran while one was open for 0% of the time, Pallas kernels for 2%

profile of v1, /device:TPU:0, one launch (start us, length us, event | category | flops | bytes accessed | tf_op | source)
XLA Modules:
  0.0 203.8 jit_solution(3137892488408490698)
XLA Ops:
  7.2 0.0 all-gather.6.cloned.1.call-start
  7.2 1.5 pad_maximum_fusion
  8.8 0.0 all-gather.6.cloned.1.call-update
  8.8 0.0 all-gather.4.cloned.1.call-start
  8.8 0.7 all-gather.4.cloned.1.call-update
  9.5 0.0 reduce-scatter.2.cloned.1.call-start
  9.6 48.4 %all-gather.6.cloned.1.call-done = bf16[4096,256]{1,0:T(8,128)(2,1)} async-done(((bf16[256,256]{1,0:T(8,128)(2,1)}), bf16[4096,256]{1,0:T(8,128)(2,1)}) %all-gather.6.cloned.1.call-update) | async-done | bytes 2097168 | tf_op jit(solution)/shard_map/all_gather | solution.py:240
  58.0 0.0 copy-start
  58.0 1.6 copy-done
  59.6 0.0 copy-start.3
  59.6 1.0 copy-done.3
  60.6 0.0 copy-start.7
  60.6 0.7 copy-done.7
  61.3 5.0 %attend.1 = (bf16[256,1024]{1,0:T(8,128)(2,1)}, f32[16,8,256]{2,1,0:T(8,128)S(1)}, bf16[16,256,2048]{2,1,0:T(8,128)(2,1)}) custom-call(s32[16]{0:T(128)S(1)} %copy-done.7, bf16[256,1024]{1,0:T(8,128)(2,1)S(1)} %copy-done.3, bf16[16,256,256]{2,1,0:T(8,128)(2,1)S(1)} %bitcast.4), custom_call_target="tpu_custom_call" | custom-call | flops 2000000000 | bytes 8388608 | tf_op jit(solution)/shard_map/attend/pallas_call | solution.py:122
  66.3 0.0 copy-start.1
  66.3 0.0 copy-start.4
  66.3 0.0 copy-start.5
  66.3 0.0 copy-start.8
  66.3 25.1 %all-gather.4.cloned.1.call-done = bf16[256,8192]{1,0:T(8,128)(2,1)} async-done(((bf16[256,1024]{1,0:T(8,128)(2,1)}), bf16[256,8192]{1,0:T(8,128)(2,1)}) %all-gather.4.cloned.1.call-update) | async-done | bytes 4194320 | tf_op jit(solution)/shard_map/all_gather | solution.py:241
  91.5 12.4 %convolution_convert_fusion.grad_ref = bf16[256,1024]{1,0:T(8,128)(2,1)} fusion(bf16[256,8192]{1,0:T(8,128)(2,1)} %all-gather.4.cloned.1.call-done, bf16[1024,8192]{1,0:T(8,128)(2,1)} %param.10), kind=kOutput, calls=%fused_computation | convolution fusion | flops 4295229440 | bytes 21495808 | tf_op jit(solution)/shard_map/rn,hn->rh/dot_general | solution.py:243
  103.8 0.0 copy-done.1
  103.8 0.0 copy-done.4
  103.8 0.0 copy-done.5
  103.8 0.0 copy-done.8
  103.8 0.0 copy-start.6
  103.8 1.0 copy-done.6
  104.9 5.2 %attend_grads.1 = (bf16[256,1024]{1,0:T(8,128)(2,1)}, bf16[16,256,256]{2,1,0:T(8,128)(2,1)S(1)}) custom-call(s32[16]{0:T(128)S(1)} %copy-done.8, bf16[256,1024]{1,0:T(8,128)(2,1)S(1)} %copy-done.4, bf16[256,1024]{1,0:T(8,128)(2,1)S(1)} %copy-done.6, bf16[256,1024]{1,0:T(8,128)(2,1)S(1)} %copy-done.5, f32[16,8,256]{2,1,0:T(8,128)S(1)} %get-tuple-element.10.factor_ref, ...), custom_call_target="tpu_custom_call" | custom-call | flops 4000000000 | bytes 8388608 | tf_op jit(solution)/shard_map/attend_grads/pallas_call | solution.py:215
  110.1 0.0 copy-start.2
  110.1 1.3 copy-done.2
  111.4 0.0 reduce-scatter.2.cloned.1.call-update
  111.5 84.3 %reduce-scatter.2.cloned.1.call-done = bf16[256,256]{1,0:T(8,128)(2,1)} async-done(((bf16[4096,256]{1,0:T(8,128)(2,1)}), bf16[256,256]{1,0:T(8,128)(2,1)}) %reduce-scatter.2.cloned.1.call-update) | async-done | bytes 131088 | tf_op jit(solution)/shard_map/reduce_scatter | solution.py:247
  195.7 1.5 fusion
Async XLA Ops:
  7.2 50.8 %all-gather.6.cloned.1.call-start = ((), (), s32[]{:S(2)}) async-start(), calls=%async_computation.3 | async-start | bytes 2228224 | tf_op jit(solution)/shard_map/all_gather | solution.py:240
  8.8 82.7 %all-gather.4.cloned.1.call-start = ((), (), s32[]{:S(2)}) async-start(), calls=%async_computation.1 | async-start | bytes 4718592 | tf_op jit(solution)/shard_map/all_gather | solution.py:241
  9.5 186.2 %reduce-scatter.2.cloned.1.call-start = ((), (), s32[]{:S(2)}) async-start(), calls=%async_computation.2 | async-start | bytes 2228224 | tf_op jit(solution)/shard_map/reduce_scatter | solution.py:247
  58.0 1.6 copy-start
  59.6 1.0 copy-start.3
  60.6 0.7 copy-start.7
  66.3 37.5 %copy-start.1 = (bf16[4096,256]{1,0:T(8,128)(2,1)S(1)}, bf16[4096,256]{1,0:T(8,128)(2,1)}, u32[]{:S(2)}) copy-start(bf16[4096,256]{1,0:T(8,128)(2,1)} %all-gather.6.cloned.1.call-done) | copy-start | bytes 6291460
  66.3 37.5 %copy-start.4 = (bf16[256,1024]{1,0:T(8,128)(2,1)S(1)}, bf16[256,1024]{1,0:T(8,128)(2,1)}, u32[]{:S(2)}) copy-start(bf16[256,1024]{1,0:T(8,128)(2,1)} %q_ref.3) | copy-start | bytes 1572868
  66.3 37.5 %copy-start.5 = (bf16[256,1024]{1,0:T(8,128)(2,1)S(1)}, bf16[256,1024]{1,0:T(8,128)(2,1)}, u32[]{:S(2)}) copy-start(bf16[256,1024]{1,0:T(8,128)(2,1)} %get-tuple-element.5.out_ref) | copy-start | bytes 1572868
  66.3 37.5 %copy-start.8 = (s32[16]{0:T(128)S(1)}, s32[16]{0:T(128)}, u32[]{:S(2)}) copy-start(s32[16]{0:T(128)} %parent_ref.3) | copy-start | bytes 196
  103.8 1.0 copy-start.6
  110.1 1.3 copy-start.2
Sparse Core Ops, SparseCore 0:
  10.7 47.2 all-gather.5
  59.7 31.7 all-gather.3
  111.6 84.1 reduce-scatter.1

commit v2 on v1

v2 whole, which is shorter than its diff:
```python
import functools
import math

import jax
import jax.numpy as jnp
from jax import lax
from jax.experimental import pallas as pl
from jax.experimental.pallas import tpu as pltpu
from jax.sharding import PartitionSpec as P

HEAD_DIM = 128
SEG = 256
NODES = 16
SIDE = 4
GROUP = 8
SCALE = 1.0 / math.sqrt(HEAD_DIM)
EXP2_SCALE = SCALE * math.log2(math.e)
NEG_FLOOR = -1e30
VMEM_LIMIT = 60 * 1024 * 1024
DEEP = 2 * HEAD_DIM
TILE = 16
SUM_LIMIT = 2.0**30

NT = (((1,), (1,)), ((), ()))
NN = (((1,), (0,)), ((), ()))


def matmul(left, right, dims=NN):
    return lax.dot_general(left, right, dims, preferred_element_type=jnp.float32)


def list_visible(parent_ref, own, visible_ref):
    visible_ref[0] = own

    def climb(state):
        node, count = state
        above = parent_ref[node]
        visible_ref[count] = above
        return above, count + 1

    def has_parent(state):
        node, count = state
        return jnp.logical_and(parent_ref[node] >= 0, count < NODES)

    return lax.while_loop(has_parent, climb, (own, jnp.int32(1)))[1]


def ring(count, shift):
    return [(i, (i + shift) % count) for i in range(count)]


def along_x(shift):
    return [(y * SIDE + x, y * SIDE + (x + shift) % SIDE) for y in range(SIDE) for x in range(SIDE)]


def along_y(shift):
    return [(y * SIDE + x, ((y + shift) % SIDE) * SIDE + x) for y in range(SIDE) for x in range(SIDE)]


def offsets(own, node):
    behind_y = lax.rem(lax.div(own, SIDE) - lax.div(node, SIDE) + SIDE, SIDE)
    behind_x = lax.rem(lax.rem(own, SIDE) - lax.rem(node, SIDE) + SIDE, SIDE)
    return behind_y, behind_x


def start_kv(i, own, visible_ref, key_refs, value_refs, key_buf, value_buf, kv_sem):
    node = visible_ref[i]
    behind_y, behind_x = offsets(own, node)
    for step in range(SIDE):

        @pl.when(behind_y == step)
        def _():
            source = key_refs[step].at[behind_x]
            pltpu.make_async_copy(source, key_buf.at[i, :, pl.ds(0, HEAD_DIM)], kv_sem.at[0, i]).start()

        @pl.when(behind_x == step)
        def _():
            source = value_refs[step].at[behind_y]
            pltpu.make_async_copy(source, value_buf.at[i, :, pl.ds(0, HEAD_DIM)], kv_sem.at[1, i]).start()


def wait_kv(i, key_refs, value_refs, key_buf, value_buf, kv_sem):
    lanes = pl.ds(0, HEAD_DIM)
    pltpu.make_async_copy(key_refs[0].at[0], key_buf.at[i, :, lanes], kv_sem.at[0, i]).wait()
    pltpu.make_async_copy(value_refs[0].at[0], value_buf.at[i, :, lanes], kv_sem.at[1, i]).wait()


def repeat(first, last, do):
    def step(i, unused):
        do(i)
        return unused

    lax.fori_loop(first, last, step, 0)


def head(h):
    return slice(h * HEAD_DIM, (h + 1) * HEAD_DIM)


def head_rows(h):
    return slice(h * SEG, (h + 1) * SEG)


def unit_lanes(count):
    lane = lax.broadcasted_iota(jnp.int32, (SEG, HEAD_DIM), 1)
    return jnp.where(lane < count, 1.0, 0.0).astype(jnp.bfloat16)


def top_rows(rows):
    place = lax.broadcasted_iota(jnp.int32, (TILE, SEG), 0)
    tile = jnp.zeros((TILE, SEG), jnp.float32)
    for n, row in enumerate(rows):
        tile = jnp.where(place == n, row, tile)
    return tile.astype(jnp.bfloat16)


def rounded(values):
    return values.astype(jnp.bfloat16).astype(jnp.float32)


def forward_kernel(
    parent_ref, q_hbm, k0, k1, k2, k3, v0, v1, v2, v3, out_hbm, out_t_hbm, inverse_ref, weights_hbm,
    visible_ref, q_ref, q_deep_ref, out_ref, out_t_ref, key_buf, value_buf, values_t_ref, weights_buf,
    score_ref, acc_ref, max_ref, kv_sem, weights_sem, one_sem,
):
    key_refs, value_refs = (k0, k1, k2, k3), (v0, v1, v2, v3)
    own = lax.axis_index("branch")
    q_copy = pltpu.make_async_copy(q_hbm, q_ref, one_sem.at[0])
    q_copy.start()
    count = list_visible(parent_ref, own, visible_ref)
    repeat(0, count, lambda i: start_kv(i, own, visible_ref, key_refs, value_refs, key_buf, value_buf, kv_sem))

    def fill(i):
        key_buf[i, :, HEAD_DIM:] = unit_lanes(1)

    repeat(0, count, fill)
    values_t_ref[HEAD_DIM:, :] = jnp.ones((TILE, SEG), jnp.bfloat16)
    q_deep_ref[:, HEAD_DIM:, :] = jnp.zeros((GROUP, HEAD_DIM, SEG), jnp.bfloat16)
    q_copy.wait()
    for h in range(GROUP):
        q_deep_ref[h, :HEAD_DIM, :] = q_ref[:, head(h)].T

    def weights_copy(i):
        return pltpu.make_async_copy(weights_buf.at[i], weights_hbm.at[i], weights_sem.at[i])

    def set_shift(h, row):
        q_deep_ref[h, HEAD_DIM : HEAD_DIM + TILE, :] = top_rows([-row])

    def own_scores(h):
        key_pos = lax.broadcasted_iota(jnp.int32, (SEG, SEG), 0)
        row_pos = lax.broadcasted_iota(jnp.int32, (SEG, SEG), 1)
        return jnp.where(key_pos <= row_pos, matmul(key_buf[0], q_deep_ref[h]), NEG_FLOOR)

    def values_in(i):
        values_t_ref[:HEAD_DIM, :] = value_buf[i, :, :HEAD_DIM].T

    def block(i):
        values_in(i)
        for h in range(GROUP):
            weights = jnp.exp2(matmul(key_buf[i], q_deep_ref[h]) * EXP2_SCALE)
            weights_buf[i, :, head_rows(h)] = weights.astype(jnp.bfloat16)
        for h in range(GROUP):
            acc_ref[h] += matmul(values_t_ref[...], weights_buf[i, :, head_rows(h)])
        weights_copy(i).start()

    def own_block(scores_of):
        values_in(0)
        for h in range(GROUP):
            weights = jnp.exp2(scores_of(h) * EXP2_SCALE)
            weights_buf[0, :, head_rows(h)] = weights.astype(jnp.bfloat16)
        for h in range(GROUP):
            acc_ref[h] = matmul(values_t_ref[...], weights_buf[0, :, head_rows(h)])
        weights_copy(0).start()

    wait_kv(0, key_refs, value_refs, key_buf, value_buf, kv_sem)
    for h in range(GROUP):
        scores = own_scores(h)
        score_ref[h] = scores
        max_ref[h : h + 1, :] = rounded(jnp.max(scores, axis=0, keepdims=True))
    for h in range(GROUP):
        set_shift(h, max_ref[h : h + 1, :])
    own_block(lambda h: score_ref[h] - max_ref[h : h + 1, :])

    def first_visit(i):
        wait_kv(i, key_refs, value_refs, key_buf, value_buf, kv_sem)
        block(i)

    repeat(1, count, first_visit)
    sums = acc_ref[:, HEAD_DIM, :]
    too_large = jnp.max(jnp.where(sums < SUM_LIMIT, 0.0, 1.0)) > 0.0

    @pl.when(too_large)
    def _():
        repeat(0, count, lambda i: weights_copy(i).wait())
        for h in range(GROUP):
            set_shift(h, jnp.zeros((1, SEG), jnp.float32))

        def raise_max(i):
            for h in range(GROUP):
                block_max = jnp.max(matmul(key_buf[i], q_deep_ref[h]), axis=0, keepdims=True)
                max_ref[h : h + 1, :] = jnp.maximum(max_ref[h : h + 1, :], block_max)

        repeat(1, count, raise_max)
        for h in range(GROUP):
            set_shift(h, rounded(max_ref[h : h + 1, :]))
        own_block(own_scores)
        repeat(1, count, block)

    inverse = 1.0 / acc_ref[:, HEAD_DIM, :]
    inverse_ref[...] = inverse
    for h in range(GROUP):
        out = acc_ref[h, :HEAD_DIM, :] * inverse[h : h + 1, :]
        out_t_ref[head(h), :] = out.astype(jnp.bfloat16)
        out_ref[:, head(h)] = out.T.astype(jnp.bfloat16)
    copies = [
        pltpu.make_async_copy(out_ref, out_hbm, one_sem.at[1]),
        pltpu.make_async_copy(out_t_ref, out_t_hbm, one_sem.at[2]),
    ]
    for copy in copies:
        copy.start()
    repeat(0, count, lambda i: weights_copy(i).wait())
    for copy in copies:
        copy.wait()


SMEM_SPEC = pl.BlockSpec(memory_space=pltpu.SMEM)
VMEM_SPEC = pl.BlockSpec(memory_space=pltpu.VMEM)
HBM_SPEC = pl.BlockSpec(memory_space=pl.ANY)
WIDTH = GROUP * HEAD_DIM


def bf16(*shape):
    return jax.ShapeDtypeStruct(shape, jnp.bfloat16)


def vmem16(*shape):
    return pltpu.VMEM(shape, jnp.bfloat16)


def vmem32(*shape):
    return pltpu.VMEM(shape, jnp.float32)


def forward(parent, queries, key_rows, value_rows):
    return pl.pallas_call(
        forward_kernel,
        out_shape=(
            bf16(SEG, WIDTH),
            bf16(WIDTH, SEG),
            jax.ShapeDtypeStruct((GROUP, SEG), jnp.float32),
            bf16(NODES, SEG, GROUP * SEG),
        ),
        in_specs=[SMEM_SPEC] + [HBM_SPEC] * 9,
        out_specs=(HBM_SPEC, HBM_SPEC, VMEM_SPEC, HBM_SPEC),
        scratch_shapes=[
            pltpu.SMEM((NODES,), jnp.int32),
            vmem16(SEG, WIDTH),
            vmem16(GROUP, DEEP, SEG),
            vmem16(SEG, WIDTH),
            vmem16(WIDTH, SEG),
            vmem16(NODES, SEG, DEEP),
            vmem16(NODES, SEG, DEEP),
            vmem16(HEAD_DIM + TILE, SEG),
            vmem16(NODES, SEG, GROUP * SEG),
            vmem32(GROUP, SEG, SEG),
            vmem32(GROUP, HEAD_DIM + TILE, SEG),
            vmem32(GROUP, SEG),
            pltpu.SemaphoreType.DMA((2, NODES)),
            pltpu.SemaphoreType.DMA((NODES,)),
            pltpu.SemaphoreType.DMA((3,)),
        ],
        compiler_params=pltpu.CompilerParams(vmem_limit_bytes=VMEM_LIMIT),
        cost_estimate=pl.CostEstimate(flops=2 * 10**9, bytes_accessed=8 * 2**20, transcendentals=3 * 10**6),
        name="attend",
    )(parent, queries, *key_rows, *value_rows)


def backward_kernel(
    parent_ref, q_hbm, grad_t_hbm, out_t_hbm, inverse_ref, k0, k1, k2, k3, v0, v1, v2, v3, weights_hbm,
    dq_hbm, dk0, dk1, dk2, dk3, dv0, dv1, dv2, dv3,
    visible_ref, q_ref, grad_t_ref, out_t_ref, q_tall_ref, grad_tall_ref, grad_deep_ref, dq_ref,
    key_buf, value_buf, weights_buf, dscore_ref, dk_ref, dv_ref, dq_acc, kv_sem, weights_sem, one_sem,
):
    key_refs, value_refs = (k0, k1, k2, k3), (v0, v1, v2, v3)
    own = lax.axis_index("branch")
    loads = [
        pltpu.make_async_copy(source, target, one_sem.at[n])
        for n, (source, target) in enumerate(((grad_t_hbm, grad_t_ref), (out_t_hbm, out_t_ref), (q_hbm, q_ref)))
    ]
    for load in loads:
        load.start()
    count = list_visible(parent_ref, own, visible_ref)

    def weights_copy(i):
        return pltpu.make_async_copy(weights_hbm.at[i], weights_buf.at[i], weights_sem.at[i])

    def start(i):
        start_kv(i, own, visible_ref, key_refs, value_refs, key_buf, value_buf, kv_sem)
        weights_copy(i).start()

    repeat(0, count, start)

    def fill(i):
        value_buf[i, :, HEAD_DIM:] = unit_lanes(3)

    repeat(0, count, fill)
    dk_ref[...] = jnp.zeros_like(dk_ref)
    dv_ref[...] = jnp.zeros_like(dv_ref)
    dq_acc[...] = jnp.zeros_like(dq_acc)
    grad_deep_ref[:, HEAD_DIM:, :] = jnp.zeros((GROUP, HEAD_DIM, SEG), jnp.bfloat16)
    for load in loads:
        load.wait()
    for h in range(GROUP):
        grad_t = (grad_t_ref[head(h), :].astype(jnp.float32) * inverse_ref[h : h + 1, :]).astype(jnp.bfloat16)
        grad_deep_ref[h, :HEAD_DIM, :] = grad_t
        grad_tall_ref[head_rows(h), :] = grad_t.T
        q_tall_ref[head_rows(h), :] = q_ref[:, head(h)]
        products = grad_t.astype(jnp.float32) * out_t_ref[head(h), :].astype(jnp.float32)
        delta = -jnp.sum(products, axis=0, keepdims=True)
        high = rounded(delta)
        middle = rounded(delta - high)
        grad_deep_ref[h, HEAD_DIM : HEAD_DIM + TILE, :] = top_rows([high, middle, delta - high - middle])

    def block(i):
        wait_kv(i, key_refs, value_refs, key_buf, value_buf, kv_sem)
        weights_copy(i).wait()
        keys_t = key_buf[i, :, :HEAD_DIM].T
        for h in range(GROUP):
            lowered = matmul(value_buf[i], grad_deep_ref[h])
            weights = weights_buf[i, :, head_rows(h)].astype(jnp.float32)
            dscore_ref[:, head_rows(h)] = (weights * lowered).astype(jnp.bfloat16)
        behind_y, behind_x = offsets(own, visible_ref[i])
        value_grad = matmul(weights_buf[i], grad_tall_ref[...])
        dv_ref[behind_x, behind_y] = value_grad.astype(jnp.bfloat16)
        key_grad = matmul(dscore_ref[...], q_tall_ref[...])
        dk_ref[behind_y, behind_x] = (key_grad * SCALE).astype(jnp.bfloat16)
        dq_acc[...] += matmul(keys_t, dscore_ref[...])

    repeat(0, count, block)
    stores = [
        pltpu.make_async_copy(dk_ref.at[n], target, kv_sem.at[0, n]) for n, target in enumerate((dk0, dk1, dk2, dk3))
    ] + [
        pltpu.make_async_copy(dv_ref.at[n], target, kv_sem.at[1, n]) for n, target in enumerate((dv0, dv1, dv2, dv3))
    ]
    for store in stores:
        store.start()
    for h in range(GROUP):
        dq_ref[:, head(h)] = (dq_acc[:, head_rows(h)] * SCALE).T.astype(jnp.bfloat16)
    dq_copy = pltpu.make_async_copy(dq_ref, dq_hbm, one_sem.at[0])
    dq_copy.start()
    for store in stores:
        store.wait()
    dq_copy.wait()


def backward(parent, queries, grad_t, out_t, inverse, key_rows, value_rows, weights):
    return pl.pallas_call(
        backward_kernel,
        out_shape=(bf16(SEG, WIDTH),) + (bf16(SIDE, SEG, HEAD_DIM),) * 8,
        in_specs=[SMEM_SPEC, HBM_SPEC, HBM_SPEC, HBM_SPEC, VMEM_SPEC] + [HBM_SPEC] * 9,
        out_specs=(HBM_SPEC,) * 9,
        scratch_shapes=[
            pltpu.SMEM((NODES,), jnp.int32),
            vmem16(SEG, WIDTH),
            vmem16(WIDTH, SEG),
            vmem16(WIDTH, SEG),
            vmem16(GROUP * SEG, HEAD_DIM),
            vmem16(GROUP * SEG, HEAD_DIM),
            vmem16(GROUP, DEEP, SEG),
            vmem16(SEG, WIDTH),
            vmem16(NODES, SEG, DEEP),
            vmem16(NODES, SEG, DEEP),
            vmem16(NODES, SEG, GROUP * SEG),
            vmem16(SEG, GROUP * SEG),
            vmem16(SIDE, SIDE, SEG, HEAD_DIM),
            vmem16(SIDE, SIDE, SEG, HEAD_DIM),
            vmem32(HEAD_DIM, GROUP * SEG),
            pltpu.SemaphoreType.DMA((2, NODES)),
            pltpu.SemaphoreType.DMA((NODES,)),
            pltpu.SemaphoreType.DMA((3,)),
        ],
        compiler_params=pltpu.CompilerParams(vmem_limit_bytes=VMEM_LIMIT),
        cost_estimate=pl.CostEstimate(flops=4 * 10**9, bytes_accessed=8 * 2**20, transcendentals=0),
        name="attend_grads",
    )(parent, queries, grad_t, out_t, inverse, *key_rows, *value_rows, weights)


def project_kernel(x_hbm, w_hbm, out_hbm, x_ref, w_ref, acc_ref, out_ref, x_sem, w_sem, out_sem):
    parts, _, width = x_ref.shape
    blocks = [slice(n * SEG, (n + 1) * SEG) for n in range(w_hbm.shape[0] // SEG)]

    def x_copy(t):
        return pltpu.make_async_copy(x_hbm.at[t], x_ref.at[t], x_sem.at[t])

    def w_copy(t, n):
        rows = pl.ds(n * SEG, SEG)
        return pltpu.make_async_copy(w_hbm.at[rows, pl.ds(t * width, width)], w_ref.at[t, rows], w_sem.at[t, n])

    for t in range(parts):
        x_copy(t).start()
        for n in range(len(blocks)):
            w_copy(t, n).start()
    for t in range(parts):
        x_copy(t).wait()
        for n in range(len(blocks)):
            w_copy(t, n).wait()
        x_t = x_ref[t].T
        for rows in blocks:
            part = matmul(w_ref[t, rows], x_t)
            if t == 0:
                acc_ref[rows] = part
            elif t < parts - 1:
                acc_ref[rows] += part
            else:
                out_ref[rows] = (acc_ref[rows] + part).astype(jnp.bfloat16)
    out_copy = pltpu.make_async_copy(out_ref, out_hbm, out_sem)
    out_copy.start()
    out_copy.wait()


def project(gathered, w_out):
    parts, rows, width = gathered.shape
    heads_wide = w_out.shape[0]
    return pl.pallas_call(
        project_kernel,
        out_shape=bf16(heads_wide, rows),
        in_specs=[HBM_SPEC] * 2,
        out_specs=HBM_SPEC,
        scratch_shapes=[
            vmem16(parts, rows, width),
            vmem16(parts, heads_wide, width),
            vmem32(heads_wide, rows),
            vmem16(heads_wide, rows),
            pltpu.SemaphoreType.DMA((parts,)),
            pltpu.SemaphoreType.DMA((parts, heads_wide // SEG)),
            pltpu.SemaphoreType.DMA,
        ],
        compiler_params=pltpu.CompilerParams(vmem_limit_bytes=VMEM_LIMIT),
        cost_estimate=pl.CostEstimate(flops=4 * 10**9, bytes_accessed=20 * 2**20, transcendentals=0),
        name="project",
    )(gathered, w_out)


def permute_line(blocks, along, sign):
    came = {step: lax.ppermute(blocks[step], "branch", along(sign * step)) for step in (1, 3, 2)}
    return [came[step] for step in (1, 2, 3)]


def gather_line(block, along):
    return [block] + permute_line([block] * SIDE, along, 1)


def add_up(parts):
    total = parts[0].astype(jnp.float32)
    for part in parts[1:]:
        total = total + part.astype(jnp.float32)
    return total.astype(jnp.bfloat16)


def per_device(queries, keys, values, grad_out, w_out, parent):
    gathered = lax.all_gather(grad_out, "tensor", axis=0)
    key_line, value_line = lax.optimization_barrier(
        (jnp.stack(gather_line(keys, along_x)), jnp.stack(gather_line(values, along_y)))
    )
    key_rows, value_rows = gather_line(key_line, along_y), gather_line(value_line, along_x)
    attn_out, out_t, inverse, weights = forward(parent, queries, key_rows, value_rows)
    grad_t = project(gathered, w_out)
    grad_queries, *lines = backward(parent, queries, grad_t, out_t, inverse, key_rows, value_rows, weights)
    key_parts = permute_line(lines[:SIDE], along_y, -1)
    value_parts = permute_line(lines[SIDE:], along_x, -1)
    value_sums = add_up([lines[SIDE]] + value_parts)
    key_sums = add_up([lines[0]] + key_parts)
    key_sums, value_sums = lax.optimization_barrier((key_sums, value_sums))
    value_parts = permute_line(value_sums, along_y, -1)
    key_parts = permute_line(key_sums, along_x, -1)
    return attn_out, grad_queries, add_up([key_sums[0]] + key_parts), add_up([value_sums[0]] + value_parts)


def solution(mesh):
    return jax.shard_map(
        per_device,
        mesh=mesh,
        in_specs=(
            P("branch", "tensor"),
            P("branch", "tensor"),
            P("branch", "tensor"),
            P("branch", "tensor"),
            P("tensor", None),
            P(),
        ),
        out_specs=(P("branch", "tensor"),) * 4,
        check_vma=False,
    )
```

time: 204 us -> 120 us (0.59)
  waiting for transfers between devices: 159 us -> 28.4 us
  starting transfers between devices: 0.12 us -> 50.3 us
  matrix products: 12.4 us -> 0 us
  Pallas kernels: 10.2 us -> 21.9 us
  local copies, waits for them, and re-layouts: 7.21 us -> 0.77 us
  other arithmetic: 1.54 us -> 5.3 us
    reduce_scatter x1 -> x0, waiting for transfers between devices: 84.3 us -> none  [per_device(): lax.psum_scatter(dkv.reshape(NODES * SEG, 2 * HEAD_DIM), 'branch', scatte...]
    all_gather x2 -> x1, waiting for transfers between devices: 73.5 us -> 0.02 us  [per_device(): gathered = lax.all_gather(grad_out, 'tensor', axis=0)]
    ppermute x0 -> x24, starting transfers between devices: none -> 50.3 us  [permute_line(): lax.ppermute(blocks[step], 'branch', along(sign * step))]
    ppermute x0 -> x24, waiting for transfers between devices: none -> 27.7 us  [permute_line(): lax.ppermute(blocks[step], 'branch', along(sign * step))]
    dot_general x1 -> x0, matrix products: 12.4 us -> none  [per_device(): jnp.einsum('rn,hn->rh', grad_all, w_out, preferred_element_type=jnp.float32)]
    pallas_call x2 -> x3, Pallas kernels: 10.2 us -> 21.9 us  [the longest x1 11.1 us: project(): pl.pallas_call(project_kernel, out_shape=bf16(heads_wide, rows), in_specs...]
    unnamed x18 -> x16, local copies, waits for them, and re-layouts: 5.68 us -> 0.74 us
    convert_element_type x0 -> x4, other arithmetic: none -> 3.52 us  [add_up(): return total.astype(jnp.bfloat16)]
  transfers between devices with their start and end apart: 3 -> 25, of which waited for: 3 -> 13; matrix products, arithmetic and copies ran while one was open for 0% -> 3% of each run, Pallas kernels for 2% -> 4%
where the time goes in v2:
time: 120 us; the launch traced here: 121 us
  starting transfers between devices  50.3 us (42%)
  waiting for transfers between devices  28.4 us (24%)
  Pallas kernels  21.9 us (18%)
  between operations  14.2 us (12%)
  other arithmetic  5.3 us (4%)
    ppermute x24, starting transfers between devices, permute_line(): lax.ppermute(blocks[step], 'branch', along(sign * step))  50.3 us
    ppermute x24, waiting for transfers between devices, permute_line(): lax.ppermute(blocks[step], 'branch', along(sign * step))  27.7 us
    pallas_call x1, Pallas kernels, project(): pl.pallas_call(project_kernel, out_shape=bf16(heads_wide, rows), in_specs...  11.1 us
    pallas_call x1, Pallas kernels, backward(): pl.pallas_call(backward_kernel, out_shape=(bf16(SEG, WIDTH),) + (bf16(SID...  5.59 us
    pallas_call x1, Pallas kernels, forward(): pl.pallas_call(forward_kernel, out_shape=(bf16(SEG, WIDTH), bf16(WIDTH, S...  5.21 us
    convert_element_type x4, other arithmetic, add_up(): return total.astype(jnp.bfloat16)  3.52 us
  transfers between devices with their start and end apart: 25, of which 13 were waited for; matrix products, arithmetic and copies ran while one was open for 3% of the time, Pallas kernels for 4%

profile of v2, /device:TPU:0, one launch (start us, length us, event | category | flops | bytes accessed | tf_op | source)
XLA Modules:
  0.0 120.9 jit_solution(73763781514789661)
XLA Ops:
  7.2 0.0 all-gather.3.cloned.1.call-start
  7.2 0.7 all-gather.3.cloned.1.call-update
  7.9 1.6 %collective-permute-start = (bf16[256,128]{1,0:T(8,128)(2,1)}, bf16[256,128]{1,0:T(8,128)(2,1)S(1)}, u32[]{:S(2)}, u32[]{:S(2)}) collective-permute-start(bf16[256,128]{1,0:T(8,128)(2,1)} %param.7), channel_id=1, source_target_pairs={{0,8},{8,16},{16,24},{24,0},{32,40},{40,48},{48,56},{56,32},{64,72... | collective-permute-start | bytes 196616 | tf_op jit(solution)/shard_map/ppermute | solution.py:445
  9.5 1.7 %collective-permute-start.2 = (bf16[256,128]{1,0:T(8,128)(2,1)}, bf16[256,128]{1,0:T(8,128)(2,1)S(1)}, u32[]{:S(2)}, u32[]{:S(2)}) collective-permute-start(bf16[256,128]{1,0:T(8,128)(2,1)} %param.7), channel_id=1, source_target_pairs={{0,24},{8,0},{16,8},{24,16},{32,56},{40,32},{48,40},{56,48},{64,88... | collective-permute-start | bytes 196616 | tf_op jit(solution)/shard_map/ppermute | solution.py:445
  11.2 1.9 %collective-permute-start.1 = (bf16[256,128]{1,0:T(8,128)(2,1)}, bf16[256,128]{1,0:T(8,128)(2,1)S(1)}, u32[]{:S(2)}, u32[]{:S(2)}) collective-permute-start(bf16[256,128]{1,0:T(8,128)(2,1)} %param.7), channel_id=1, source_target_pairs={{0,16},{8,24},{16,0},{24,8},{32,48},{40,56},{48,32},{56,40},{64,80... | collective-permute-start | bytes 196616 | tf_op jit(solution)/shard_map/ppermute | solution.py:445
  13.1 1.6 %collective-permute-start.3 = (bf16[256,128]{1,0:T(8,128)(2,1)}, bf16[256,128]{1,0:T(8,128)(2,1)S(1)}, u32[]{:S(2)}, u32[]{:S(2)}) collective-permute-start(bf16[256,128]{1,0:T(8,128)(2,1)} %param.8), channel_id=1, source_target_pairs={{0,32},{8,40},{16,48},{24,56},{32,64},{40,72},{48,80},{56,88},{64,... | collective-permute-start | bytes 196616 | tf_op jit(solution)/shard_map/ppermute | solution.py:445
  14.7 1.7 %collective-permute-start.5 = (bf16[256,128]{1,0:T(8,128)(2,1)}, bf16[256,128]{1,0:T(8,128)(2,1)S(1)}, u32[]{:S(2)}, u32[]{:S(2)}) collective-permute-start(bf16[256,128]{1,0:T(8,128)(2,1)} %param.8), channel_id=1, source_target_pairs={{0,96},{8,104},{16,112},{24,120},{32,0},{40,8},{48,16},{56,24},{64... | collective-permute-start | bytes 196616 | tf_op jit(solution)/shard_map/ppermute | solution.py:445
  16.3 0.0 collective-permute-done
  16.3 2.0 %collective-permute-start.4 = (bf16[256,128]{1,0:T(8,128)(2,1)}, bf16[256,128]{1,0:T(8,128)(2,1)S(1)}, u32[]{:S(2)}, u32[]{:S(2)}) collective-permute-start(bf16[256,128]{1,0:T(8,128)(2,1)} %param.8), channel_id=1, source_target_pairs={{0,64},{8,72},{16,80},{24,88},{32,96},{40,104},{48,112},{56,120},{... | collective-permute-start | bytes 196616 | tf_op jit(solution)/shard_map/ppermute | solution.py:445
  18.3 0.0 collective-permute-done.2
  18.3 0.0 collective-permute-done.1
  18.3 0.9 pad_maximum_fusion.k0
  19.2 0.0 copy-start
  19.2 0.0 collective-permute-done.3
  19.2 0.4 collective-permute-done.5
  19.6 2.7 %collective-permute-done.4 = bf16[256,128]{1,0:T(8,128)(2,1)S(1)} collective-permute-done((bf16[256,128]{1,0:T(8,128)(2,1)}, bf16[256,128]{1,0:T(8,128)(2,1)S(1)}, u32[]{:S(2)}, u32[]{:S(2)}) %collective-permute-start.4) | collective-permute-done | bytes 65568 | tf_op jit(solution)/shard_map/ppermute | solution.py:445
  22.3 0.9 pad_maximum_fusion.1.v0
  23.2 0.0 copy-start.1
  23.2 1.8 %collective-permute-start.8 = (bf16[4,256,128]{2,1,0:T(8,128)(2,1)S(1)}, bf16[4,256,128]{2,1,0:T(8,128)(2,1)S(1)}, u32[]{:S(2)}, u32[]{:S(2)}) collective-permute-start(bf16[4,256,128]{2,1,0:T(8,128)(2,1)S(1)} %pad_maximum_fusion.k0), channel_id=1, source_target_pairs={{0,96},{8,104},{16,112},{24,120},{32,0},{40,8},{48,16},{56,24},{64... | collective-permute-start | bytes 786440 | tf_op jit(solution)/shard_map/ppermute | solution.py:445
  25.1 0.6 collective-permute-start.7
  25.7 1.0 collective-permute-start.6
  26.7 1.1 collective-permute-start.11
  27.8 1.5 %collective-permute-start.10 = (bf16[4,256,128]{2,1,0:T(8,128)(2,1)S(1)}, bf16[4,256,128]{2,1,0:T(8,128)(2,1)S(1)}, u32[]{:S(2)}, u32[]{:S(2)}) collective-permute-start(bf16[4,256,128]{2,1,0:T(8,128)(2,1)S(1)} %pad_maximum_fusion.1.v0), channel_id=1, source_target_pairs={{0,16},{8,24},{16,0},{24,8},{32,48},{40,56},{48,32},{56,40},{64,80... | collective-permute-start | bytes 786440 | tf_op jit(solution)/shard_map/ppermute | solution.py:445
  29.4 2.8 %collective-permute-done.8.k3 = bf16[4,256,128]{2,1,0:T(8,128)(2,1)S(1)} collective-permute-done((bf16[4,256,128]{2,1,0:T(8,128)(2,1)S(1)}, bf16[4,256,128]{2,1,0:T(8,128)(2,1)S(1)}, u32[]{:S(2)}, u32[]{:S(2)}) %collective-permute-start.8) | collective-permute-done | bytes 262176 | tf_op jit(solution)/shard_map/ppermute | solution.py:445
  32.2 0.6 collective-permute-start.9
  32.8 2.4 %collective-permute-done.7.k2 = bf16[4,256,128]{2,1,0:T(8,128)(2,1)S(1)} collective-permute-done((bf16[4,256,128]{2,1,0:T(8,128)(2,1)S(1)}, bf16[4,256,128]{2,1,0:T(8,128)(2,1)S(1)}, u32[]{:S(2)}, u32[]{:S(2)}) %collective-permute-start.7) | collective-permute-done | bytes 262176 | tf_op jit(solution)/shard_map/ppermute | solution.py:445
  35.2 2.4 %collective-permute-done.6.k1 = bf16[4,256,128]{2,1,0:T(8,128)(2,1)S(1)} collective-permute-done((bf16[4,256,128]{2,1,0:T(8,128)(2,1)S(1)}, bf16[4,256,128]{2,1,0:T(8,128)(2,1)S(1)}, u32[]{:S(2)}, u32[]{:S(2)}) %collective-permute-start.6) | collective-permute-done | bytes 262176 | tf_op jit(solution)/shard_map/ppermute | solution.py:445
  37.6 0.0 collective-permute-done.11.v3
  37.6 0.0 collective-permute-done.10.v2
  37.6 0.0 copy-start.6
  37.6 2.1 %collective-permute-done.9.v1 = bf16[4,256,128]{2,1,0:T(8,128)(2,1)S(1)} collective-permute-done((bf16[4,256,128]{2,1,0:T(8,128)(2,1)S(1)}, bf16[4,256,128]{2,1,0:T(8,128)(2,1)S(1)}, u32[]{:S(2)}, u32[]{:S(2)}) %collective-permute-start.9) | collective-permute-done | bytes 262176 | tf_op jit(solution)/shard_map/ppermute | solution.py:445
  39.8 0.7 copy-done.7
  40.5 5.2 %attend.1 = (bf16[256,1024]{1,0:T(8,128)(2,1)}, bf16[1024,256]{1,0:T(8,128)(2,1)}, f32[8,256]{1,0:T(8,128)}, bf16[16,256,2048]{2,1,0:T(8,128)(2,1)}) custom-call(s32[16]{0:T(128)} %parent_ref.3, bf16[256,1024]{1,0:T(8,128)(2,1)} %q_hbm.3, bf16[4,256,128]{2,1,0:T(8,128)(2,1)} %copy-done, bf16[4,256,128]{2,1,0:T(8,128)(2,1)} %copy-done.4, ...), custom_call_target="tpu_custom_call" | custom-call | flops 2000000000 | bytes 8388608 | tf_op jit(solution)/shard_map/attend/pallas_call | solution.py:245
  45.7 0.0 all-gather.3.cloned.1.call-done
  45.8 11.1 %project.1.grad_t_hbm = bf16[1024,256]{1,0:T(8,128)(2,1)} custom-call(bf16[8,256,1024]{2,1,0:T(8,128)(2,1)} %bitcast.27, bf16[1024,8192]{1,0:T(8,128)(2,1)} %w_hbm.1), custom_call_target="tpu_custom_call" | custom-call | flops 4000000000 | bytes 20971520 | tf_op jit(solution)/shard_map/project/pallas_call | solution.py:424
  56.9 5.6 %attend_grads.1 = (bf16[256,1024]{1,0:T(8,128)(2,1)}, bf16[4,256,128]{2,1,0:T(8,128)(2,1)}, bf16[4,256,128]{2,1,0:T(8,128)(2,1)}, bf16[4,256,128]{2,1,0:T(8,128)...) custom-call(s32[16]{0:T(128)} %parent_ref.3, ...), custom_call_target="tpu_custom_call" | custom-call | flops 4000000000 | bytes 8388608 | tf_op jit(solution)/shard_map/attend_grads/pallas_call | solution.py:357
  62.5 18.4 %collective-permute-start.12 = (bf16[4,256,128]{2,1,0:T(8,128)(2,1)}, bf16[4,256,128]{2,1,0:T(8,128)(2,1)S(1)}, u32[]{:S(2)}, u32[]{:S(2)}) collective-permute-start(bf16[4,256,128]{2,1,0:T(8,128)(2,1)} %get-tuple-element.29), channel_id=1, source_target_pairs={{0,96},{8,104},{16,112},{24,120},{32,0},{40,8},{48,16},{56,24},{64... | collective-permute-start | bytes 786440 | tf_op jit(solution)/shard_map/ppermute | solution.py:445
  81.0 0.0 collective-permute-start.13
  81.0 0.9 collective-permute-start.14
  81.9 5.5 %collective-permute-start.15 = (bf16[4,256,128]{2,1,0:T(8,128)(2,1)}, bf16[4,256,128]{2,1,0:T(8,128)(2,1)S(1)}, u32[]{:S(2)}, u32[]{:S(2)}) collective-permute-start(bf16[4,256,128]{2,1,0:T(8,128)(2,1)} %get-tuple-element.33), channel_id=1, source_target_pairs={{0,24},{8,0},{16,8},{24,16},{32,56},{40,32},{48,40},{56,48},{64,88... | collective-permute-start | bytes 786440 | tf_op jit(solution)/shard_map/ppermute | solution.py:445
  87.5 0.0 collective-permute-start.16
  87.5 0.5 collective-permute-done.12
  88.0 0.3 collective-permute-start.17
  88.3 0.8 collective-permute-done.13
  89.2 2.4 %collective-permute-done.14 = bf16[4,256,128]{2,1,0:T(8,128)(2,1)S(1)} collective-permute-done((bf16[4,256,128]{2,1,0:T(8,128)(2,1)}, bf16[4,256,128]{2,1,0:T(8,128)(2,1)S(1)}, u32[]{:S(2)}, u32[]{:S(2)}) %collective-permute-start.14) | collective-permute-done | bytes 262176 | tf_op jit(solution)/shard_map/ppermute | solution.py:445
  91.6 1.1 add_convert_fusion.1
  92.7 2.4 %collective-permute-done.15 = bf16[4,256,128]{2,1,0:T(8,128)(2,1)S(1)} collective-permute-done((bf16[4,256,128]{2,1,0:T(8,128)(2,1)}, bf16[4,256,128]{2,1,0:T(8,128)(2,1)S(1)}, u32[]{:S(2)}, u32[]{:S(2)}) %collective-permute-start.15) | collective-permute-done | bytes 262176 | tf_op jit(solution)/shard_map/ppermute | solution.py:445
  95.1 0.5 collective-permute-done.16
  95.6 4.2 %collective-permute-done.17 = bf16[4,256,128]{2,1,0:T(8,128)(2,1)S(1)} collective-permute-done((bf16[4,256,128]{2,1,0:T(8,128)(2,1)}, bf16[4,256,128]{2,1,0:T(8,128)(2,1)S(1)}, u32[]{:S(2)}, u32[]{:S(2)}) %collective-permute-start.17) | collective-permute-done | bytes 262176 | tf_op jit(solution)/shard_map/ppermute | solution.py:445
  99.8 1.1 add_convert_fusion
  100.9 1.1 collective-permute-start.18
  102.0 1.0 collective-permute-start.20
  103.0 0.6 collective-permute-start.19
  103.6 3.7 %collective-permute-start.21 = (bf16[256,128]{1,0:T(8,128)(2,1)S(1)}, bf16[256,128]{1,0:T(8,128)(2,1)S(1)}, u32[]{:S(2)}, u32[]{:S(2)}) collective-permute-start(bf16[256,128]{1,0:T(8,128)(2,1)S(1)} %get-tuple-element.38), channel_id=1, source_target_pairs={{0,96},{8,104},{16,112},{24,120},{32,0},{40,8},{48,16},{56,24},{64... | collective-permute-start | bytes 196616 | tf_op jit(solution)/shard_map/ppermute | solution.py:445
  107.2 0.0 collective-permute-start.23
  107.2 0.0 collective-permute-done.18
  107.2 1.5 %collective-permute-start.22 = (bf16[256,128]{1,0:T(8,128)(2,1)S(1)}, bf16[256,128]{1,0:T(8,128)(2,1)S(1)}, u32[]{:S(2)}, u32[]{:S(2)}) collective-permute-start(bf16[256,128]{1,0:T(8,128)(2,1)S(1)} %get-tuple-element.40), channel_id=1, source_target_pairs={{0,64},{8,72},{16,80},{24,88},{32,96},{40,104},{48,112},{56,120},{... | collective-permute-start | bytes 196616 | tf_op jit(solution)/shard_map/ppermute | solution.py:445
  108.8 0.0 collective-permute-done.20
  108.8 0.0 collective-permute-done.19
  108.8 0.7 fusion.5
  109.4 0.0 collective-permute-done.21
  109.4 4.0 %collective-permute-done.23 = bf16[256,128]{1,0:T(8,128)(2,1)S(1)} collective-permute-done((bf16[256,128]{1,0:T(8,128)(2,1)S(1)}, bf16[256,128]{1,0:T(8,128)(2,1)S(1)}, u32[]{:S(2)}, u32[]{:S(2)}) %collective-permute-start.23) | collective-permute-done | bytes 65568 | tf_op jit(solution)/shard_map/ppermute | solution.py:445
  113.4 0.0 collective-permute-done.22
  113.4 0.7 fusion.2
  (14 shorter events, 0.1 us)
Async XLA Ops:
  7.2 38.6 %all-gather.3.cloned.1.call-start = ((), (), s32[]{:S(2)}) async-start(), calls=%async_computation | async-start | bytes 4718592 | tf_op jit(solution)/shard_map/all_gather | solution.py:461
  7.9 8.4 %collective-permute-start = (bf16[256,128]{1,0:T(8,128)(2,1)}, bf16[256,128]{1,0:T(8,128)(2,1)S(1)}, u32[]{:S(2)}, u32[]{:S(2)}) collective-permute-start(bf16[256,128]{1,0:T(8,128)(2,1)} %param.7), channel_id=1, source_target_pairs={{0,8},{8,16},{16,24},{24,0},{32,40},{40,48},{48,56},{56,32},{64,72... | collective-permute-start | bytes 196616 | tf_op jit(solution)/shard_map/ppermute | solution.py:445
  9.5 8.8 %collective-permute-start.2 = (bf16[256,128]{1,0:T(8,128)(2,1)}, bf16[256,128]{1,0:T(8,128)(2,1)S(1)}, u32[]{:S(2)}, u32[]{:S(2)}) collective-permute-start(bf16[256,128]{1,0:T(8,128)(2,1)} %param.7), channel_id=1, source_target_pairs={{0,24},{8,0},{16,8},{24,16},{32,56},{40,32},{48,40},{56,48},{64,88... | collective-permute-start | bytes 196616 | tf_op jit(solution)/shard_map/ppermute | solution.py:445
  11.2 7.1 %collective-permute-start.1 = (bf16[256,128]{1,0:T(8,128)(2,1)}, bf16[256,128]{1,0:T(8,128)(2,1)S(1)}, u32[]{:S(2)}, u32[]{:S(2)}) collective-permute-start(bf16[256,128]{1,0:T(8,128)(2,1)} %param.7), channel_id=1, source_target_pairs={{0,16},{8,24},{16,0},{24,8},{32,48},{40,56},{48,32},{56,40},{64,80... | collective-permute-start | bytes 196616 | tf_op jit(solution)/shard_map/ppermute | solution.py:445
  13.1 6.1 %collective-permute-start.3 = (bf16[256,128]{1,0:T(8,128)(2,1)}, bf16[256,128]{1,0:T(8,128)(2,1)S(1)}, u32[]{:S(2)}, u32[]{:S(2)}) collective-permute-start(bf16[256,128]{1,0:T(8,128)(2,1)} %param.8), channel_id=1, source_target_pairs={{0,32},{8,40},{16,48},{24,56},{32,64},{40,72},{48,80},{56,88},{64,... | collective-permute-start | bytes 196616 | tf_op jit(solution)/shard_map/ppermute | solution.py:445
  14.7 4.9 %collective-permute-start.5 = (bf16[256,128]{1,0:T(8,128)(2,1)}, bf16[256,128]{1,0:T(8,128)(2,1)S(1)}, u32[]{:S(2)}, u32[]{:S(2)}) collective-permute-start(bf16[256,128]{1,0:T(8,128)(2,1)} %param.8), channel_id=1, source_target_pairs={{0,96},{8,104},{16,112},{24,120},{32,0},{40,8},{48,16},{56,24},{64... | collective-permute-start | bytes 196616 | tf_op jit(solution)/shard_map/ppermute | solution.py:445
  16.3 6.0 %collective-permute-start.4 = (bf16[256,128]{1,0:T(8,128)(2,1)}, bf16[256,128]{1,0:T(8,128)(2,1)S(1)}, u32[]{:S(2)}, u32[]{:S(2)}) collective-permute-start(bf16[256,128]{1,0:T(8,128)(2,1)} %param.8), channel_id=1, source_target_pairs={{0,64},{8,72},{16,80},{24,88},{32,96},{40,104},{48,112},{56,120},{... | collective-permute-start | bytes 196616 | tf_op jit(solution)/shard_map/ppermute | solution.py:445
  19.2 20.5 %copy-start = (bf16[4,256,128]{2,1,0:T(8,128)(2,1)}, bf16[4,256,128]{2,1,0:T(8,128)(2,1)S(1)}, u32[]{:S(2)}) copy-start(bf16[4,256,128]{2,1,0:T(8,128)(2,1)S(1)} %pad_maximum_fusion.k0) | copy-start | bytes 786436
  23.2 16.5 %copy-start.1 = (bf16[4,256,128]{2,1,0:T(8,128)(2,1)}, bf16[4,256,128]{2,1,0:T(8,128)(2,1)S(1)}, u32[]{:S(2)}) copy-start(bf16[4,256,128]{2,1,0:T(8,128)(2,1)S(1)} %pad_maximum_fusion.1.v0) | copy-start | bytes 786436
  23.2 8.9 %collective-permute-start.8 = (bf16[4,256,128]{2,1,0:T(8,128)(2,1)S(1)}, bf16[4,256,128]{2,1,0:T(8,128)(2,1)S(1)}, u32[]{:S(2)}, u32[]{:S(2)}) collective-permute-start(bf16[4,256,128]{2,1,0:T(8,128)(2,1)S(1)} %pad_maximum_fusion.k0), channel_id=1, source_target_pairs={{0,96},{8,104},{16,112},{24,120},{32,0},{40,8},{48,16},{56,24},{64... | collective-permute-start | bytes 786440 | tf_op jit(solution)/shard_map/ppermute | solution.py:445
  25.1 10.1 %collective-permute-start.7 = (bf16[4,256,128]{2,1,0:T(8,128)(2,1)S(1)}, bf16[4,256,128]{2,1,0:T(8,128)(2,1)S(1)}, u32[]{:S(2)}, u32[]{:S(2)}) collective-permute-start(bf16[4,256,128]{2,1,0:T(8,128)(2,1)S(1)} %pad_maximum_fusion.k0), channel_id=1, source_target_pairs={{0,64},{8,72},{16,80},{24,88},{32,96},{40,104},{48,112},{56,120},{... | collective-permute-start | bytes 786440 | tf_op jit(solution)/shard_map/ppermute | solution.py:445
  25.7 11.9 %collective-permute-start.6 = (bf16[4,256,128]{2,1,0:T(8,128)(2,1)S(1)}, bf16[4,256,128]{2,1,0:T(8,128)(2,1)S(1)}, u32[]{:S(2)}, u32[]{:S(2)}) collective-permute-start(bf16[4,256,128]{2,1,0:T(8,128)(2,1)S(1)} %pad_maximum_fusion.k0), channel_id=1, source_target_pairs={{0,32},{8,40},{16,48},{24,56},{32,64},{40,72},{48,80},{56,88},{64,... | collective-permute-start | bytes 786440 | tf_op jit(solution)/shard_map/ppermute | solution.py:445
  26.7 10.9 %collective-permute-start.11 = (bf16[4,256,128]{2,1,0:T(8,128)(2,1)S(1)}, bf16[4,256,128]{2,1,0:T(8,128)(2,1)S(1)}, u32[]{:S(2)}, u32[]{:S(2)}) collective-permute-start(bf16[4,256,128]{2,1,0:T(8,128)(2,1)S(1)} %pad_maximum_fusion.1.v0), channel_id=1, source_target_pairs={{0,24},{8,0},{16,8},{24,16},{32,56},{40,32},{48,40},{56,48},{64,88... | collective-permute-start | bytes 786440 | tf_op jit(solution)/shard_map/ppermute | solution.py:445
  27.8 9.8 %collective-permute-start.10 = (bf16[4,256,128]{2,1,0:T(8,128)(2,1)S(1)}, bf16[4,256,128]{2,1,0:T(8,128)(2,1)S(1)}, u32[]{:S(2)}, u32[]{:S(2)}) collective-permute-start(bf16[4,256,128]{2,1,0:T(8,128)(2,1)S(1)} %pad_maximum_fusion.1.v0), channel_id=1, source_target_pairs={{0,16},{8,24},{16,0},{24,8},{32,48},{40,56},{48,32},{56,40},{64,80... | collective-permute-start | bytes 786440 | tf_op jit(solution)/shard_map/ppermute | solution.py:445
  32.2 7.6 %copy-start.2 = (bf16[4,256,128]{2,1,0:T(8,128)(2,1)}, bf16[4,256,128]{2,1,0:T(8,128)(2,1)S(1)}, u32[]{:S(2)}) copy-start(bf16[4,256,128]{2,1,0:T(8,128)(2,1)S(1)} %collective-permute-done.8.k3) | copy-start | bytes 786436
  32.2 7.6 %collective-permute-start.9 = (bf16[4,256,128]{2,1,0:T(8,128)(2,1)S(1)}, bf16[4,256,128]{2,1,0:T(8,128)(2,1)S(1)}, u32[]{:S(2)}, u32[]{:S(2)}) collective-permute-start(bf16[4,256,128]{2,1,0:T(8,128)(2,1)S(1)} %pad_maximum_fusion.1.v0), channel_id=1, source_target_pairs={{0,8},{8,16},{16,24},{24,0},{32,40},{40,48},{48,56},{56,32},{64,72... | collective-permute-start | bytes 786440 | tf_op jit(solution)/shard_map/ppermute | solution.py:445
  35.2 4.6 %copy-start.3 = (bf16[4,256,128]{2,1,0:T(8,128)(2,1)}, bf16[4,256,128]{2,1,0:T(8,128)(2,1)S(1)}, u32[]{:S(2)}) copy-start(bf16[4,256,128]{2,1,0:T(8,128)(2,1)S(1)} %collective-permute-done.7.k2) | copy-start | bytes 786436
  37.6 2.2 %copy-start.4 = (bf16[4,256,128]{2,1,0:T(8,128)(2,1)}, bf16[4,256,128]{2,1,0:T(8,128)(2,1)S(1)}, u32[]{:S(2)}) copy-start(bf16[4,256,128]{2,1,0:T(8,128)(2,1)S(1)} %collective-permute-done.6.k1) | copy-start | bytes 786436
  37.6 2.2 %copy-start.5 = (bf16[4,256,128]{2,1,0:T(8,128)(2,1)}, bf16[4,256,128]{2,1,0:T(8,128)(2,1)S(1)}, u32[]{:S(2)}) copy-start(bf16[4,256,128]{2,1,0:T(8,128)(2,1)S(1)} %collective-permute-done.11.v3) | copy-start | bytes 786436
  37.6 2.2 %copy-start.6 = (bf16[4,256,128]{2,1,0:T(8,128)(2,1)}, bf16[4,256,128]{2,1,0:T(8,128)(2,1)S(1)}, u32[]{:S(2)}) copy-start(bf16[4,256,128]{2,1,0:T(8,128)(2,1)S(1)} %collective-permute-done.10.v2) | copy-start | bytes 786436
  39.8 0.7 copy-start.7
  62.5 25.5 %collective-permute-start.12 = (bf16[4,256,128]{2,1,0:T(8,128)(2,1)}, bf16[4,256,128]{2,1,0:T(8,128)(2,1)S(1)}, u32[]{:S(2)}, u32[]{:S(2)}) collective-permute-start(bf16[4,256,128]{2,1,0:T(8,128)(2,1)} %get-tuple-element.29), channel_id=1, source_target_pairs={{0,96},{8,104},{16,112},{24,120},{32,0},{40,8},{48,16},{56,24},{64... | collective-permute-start | bytes 786440 | tf_op jit(solution)/shard_map/ppermute | solution.py:445
  81.0 8.2 %collective-permute-start.13 = (bf16[4,256,128]{2,1,0:T(8,128)(2,1)}, bf16[4,256,128]{2,1,0:T(8,128)(2,1)S(1)}, u32[]{:S(2)}, u32[]{:S(2)}) collective-permute-start(bf16[4,256,128]{2,1,0:T(8,128)(2,1)} %get-tuple-element.30), channel_id=1, source_target_pairs={{0,64},{8,72},{16,80},{24,88},{32,96},{40,104},{48,112},{56,120},{... | collective-permute-start | bytes 786440 | tf_op jit(solution)/shard_map/ppermute | solution.py:445
  81.0 10.6 %collective-permute-start.14 = (bf16[4,256,128]{2,1,0:T(8,128)(2,1)}, bf16[4,256,128]{2,1,0:T(8,128)(2,1)S(1)}, u32[]{:S(2)}, u32[]{:S(2)}) collective-permute-start(bf16[4,256,128]{2,1,0:T(8,128)(2,1)} %get-tuple-element.31), channel_id=1, source_target_pairs={{0,32},{8,40},{16,48},{24,56},{32,64},{40,72},{48,80},{56,88},{64,... | collective-permute-start | bytes 786440 | tf_op jit(solution)/shard_map/ppermute | solution.py:445
  81.9 13.1 %collective-permute-start.15 = (bf16[4,256,128]{2,1,0:T(8,128)(2,1)}, bf16[4,256,128]{2,1,0:T(8,128)(2,1)S(1)}, u32[]{:S(2)}, u32[]{:S(2)}) collective-permute-start(bf16[4,256,128]{2,1,0:T(8,128)(2,1)} %get-tuple-element.33), channel_id=1, source_target_pairs={{0,24},{8,0},{16,8},{24,16},{32,56},{40,32},{48,40},{56,48},{64,88... | collective-permute-start | bytes 786440 | tf_op jit(solution)/shard_map/ppermute | solution.py:445
  87.5 8.1 %collective-permute-start.16 = (bf16[4,256,128]{2,1,0:T(8,128)(2,1)}, bf16[4,256,128]{2,1,0:T(8,128)(2,1)S(1)}, u32[]{:S(2)}, u32[]{:S(2)}) collective-permute-start(bf16[4,256,128]{2,1,0:T(8,128)(2,1)} %get-tuple-element.34), channel_id=1, source_target_pairs={{0,16},{8,24},{16,0},{24,8},{32,48},{40,56},{48,32},{56,40},{64,80... | collective-permute-start | bytes 786440 | tf_op jit(solution)/shard_map/ppermute | solution.py:445
  88.0 11.8 %collective-permute-start.17 = (bf16[4,256,128]{2,1,0:T(8,128)(2,1)}, bf16[4,256,128]{2,1,0:T(8,128)(2,1)S(1)}, u32[]{:S(2)}, u32[]{:S(2)}) collective-permute-start(bf16[4,256,128]{2,1,0:T(8,128)(2,1)} %get-tuple-element.35), channel_id=1, source_target_pairs={{0,8},{8,16},{16,24},{24,0},{32,40},{40,48},{48,56},{56,32},{64,72... | collective-permute-start | bytes 786440 | tf_op jit(solution)/shard_map/ppermute | solution.py:445
  100.9 6.3 %collective-permute-start.18 = (bf16[256,128]{1,0:T(8,128)(2,1)S(1)}, bf16[256,128]{1,0:T(8,128)(2,1)S(1)}, u32[]{:S(2)}, u32[]{:S(2)}) collective-permute-start(bf16[256,128]{1,0:T(8,128)(2,1)S(1)} %get-tuple-element.41), channel_id=1, source_target_pairs={{0,24},{8,0},{16,8},{24,16},{32,56},{40,32},{48,40},{56,48},{64,88... | collective-permute-start | bytes 196616 | tf_op jit(solution)/shard_map/ppermute | solution.py:445
  102.0 6.8 %collective-permute-start.20 = (bf16[256,128]{1,0:T(8,128)(2,1)S(1)}, bf16[256,128]{1,0:T(8,128)(2,1)S(1)}, u32[]{:S(2)}, u32[]{:S(2)}) collective-permute-start(bf16[256,128]{1,0:T(8,128)(2,1)S(1)} %get-tuple-element.42), channel_id=1, source_target_pairs={{0,8},{8,16},{16,24},{24,0},{32,40},{40,48},{48,56},{56,32},{64,72... | collective-permute-start | bytes 196616 | tf_op jit(solution)/shard_map/ppermute | solution.py:445
  103.0 5.8 %collective-permute-start.19 = (bf16[256,128]{1,0:T(8,128)(2,1)S(1)}, bf16[256,128]{1,0:T(8,128)(2,1)S(1)}, u32[]{:S(2)}, u32[]{:S(2)}) collective-permute-start(bf16[256,128]{1,0:T(8,128)(2,1)S(1)} %get-tuple-element.43), channel_id=1, source_target_pairs={{0,16},{8,24},{16,0},{24,8},{32,48},{40,56},{48,32},{56,40},{64,80... | collective-permute-start | bytes 196616 | tf_op jit(solution)/shard_map/ppermute | solution.py:445
  103.6 5.9 %collective-permute-start.21 = (bf16[256,128]{1,0:T(8,128)(2,1)S(1)}, bf16[256,128]{1,0:T(8,128)(2,1)S(1)}, u32[]{:S(2)}, u32[]{:S(2)}) collective-permute-start(bf16[256,128]{1,0:T(8,128)(2,1)S(1)} %get-tuple-element.38), channel_id=1, source_target_pairs={{0,96},{8,104},{16,112},{24,120},{32,0},{40,8},{48,16},{56,24},{64... | collective-permute-start | bytes 196616 | tf_op jit(solution)/shard_map/ppermute | solution.py:445
  107.2 6.2 %collective-permute-start.23 = (bf16[256,128]{1,0:T(8,128)(2,1)S(1)}, bf16[256,128]{1,0:T(8,128)(2,1)S(1)}, u32[]{:S(2)}, u32[]{:S(2)}) collective-permute-start(bf16[256,128]{1,0:T(8,128)(2,1)S(1)} %get-tuple-element.39), channel_id=1, source_target_pairs={{0,32},{8,40},{16,48},{24,56},{32,64},{40,72},{48,80},{56,88},{64,... | collective-permute-start | bytes 196616 | tf_op jit(solution)/shard_map/ppermute | solution.py:445
  107.2 6.2 %collective-permute-start.22 = (bf16[256,128]{1,0:T(8,128)(2,1)S(1)}, bf16[256,128]{1,0:T(8,128)(2,1)S(1)}, u32[]{:S(2)}, u32[]{:S(2)}) collective-permute-start(bf16[256,128]{1,0:T(8,128)(2,1)S(1)} %get-tuple-element.40), channel_id=1, source_target_pairs={{0,64},{8,72},{16,80},{24,88},{32,96},{40,104},{48,112},{56,120},{... | collective-permute-start | bytes 196616 | tf_op jit(solution)/shard_map/ppermute | solution.py:445
Sparse Core Ops, SparseCore 0:
  9.7 34.7 all-gather.2
